TPU v7x, 32 devices: a whole 2x2x4 slice. The times are simulated.
32 devices in a mesh: cell: 8 (over z, y), sensor: 4 (over x, core).
Axes of the slice: x: 2, y: 2, z: 4, core: 2. Of those that a mesh axis runs over, the one named last changes fastest.
Arguments:
- kernel: bfloat16 [2, 65, 256, 2048], P(None, None, 'sensor', 'cell'), may hold values from -3 to 3
- observed: float32 [64, 256], P(None, 'sensor'), may hold values from -6 to 6
- start_model: float32 [64, 2048], P(None, 'cell'), may hold values from -6 to 6
- start_multiplier: float32 [4, 64, 2048], P(None, None, 'cell'), may hold values from -1.8 to 1.8
- neighbours: int32 [4, 2048], P(None, 'cell'), may hold values from 0 to 2047, as said below
- tile_of_cell: int32 [2048], P('cell'), may hold values from 0 to 63
- tile_weight: float32 [64], replicated, may hold values from 0.3 to 3
Outputs:
- estimate: float32 [64, 2048], P(None, 'cell')
- auxiliary: float32 [4, 64, 2048], P(None, None, 'cell')
- multiplier: float32 [4, 64, 2048], P(None, None, 'cell')
Inputs may be any that keep to these rules, and one draw needn't show every extreme that they name: The cells form a grid of 16 rows of 128 cells, numbered row by row. neighbours[k, c] is c itself or the cell beside c: c + 1 for k = 0 and c - 1 for k = 1 within the same row, c - 128 for k = 2 and c + 128 for k = 3. Where neighbours[k, c] = c' differs from c, neighbours[k xor 1, c'] = c.
All inputs are finite; a program needn't handle non-finite values.
Results may differ from a plain program's by a relative error of at most 0.00092.
Values sent between devices are 32-bit elements; how exact they have to be, the bound alone decides.
No kernel may reach another device: no remote copies, remote signals or barrier semaphores. Data moves between devices by JAX's collectives and lax.ppermute only.
A program may use at most 64 MiB of HBM per device.

v0:
```python
import jax
import jax.numpy as jnp
from jax import lax
from jax.sharding import PartitionSpec as P

COLS = 128
ITERS = 2


SHRINK_SCALE = 0.4
TINY = 1e-06


def padded_2(array, sides, width):
    for axis, dim in sides:
        devices, length = (lax.axis_size(axis), array.shape[dim])
        up = [(i, (i + 1) % devices) for i in range(devices - 1)]
        down = [(j, i) for i, j in up]
        last = lax.slice_in_dim(array, length - width, length, axis=dim)
        leading = lax.slice_in_dim(array, 0, width, axis=dim)
        before = lax.ppermute(last, axis, up)
        after = lax.ppermute(leading, axis, down)
        array = jnp.concatenate([before, array, after], axis=dim)
    return array


def exact_dot(left, right):
    return jnp.dot(left, right, precision=lax.Precision.HIGHEST, preferred_element_type=jnp.float32)


def tables(times_count, freq_count):
    padded = 2 * times_count
    freq_index = lax.broadcasted_iota(jnp.int32, (freq_count, times_count), 0)
    time_index = lax.broadcasted_iota(jnp.int32, (freq_count, times_count), 1)
    phase = (freq_index * time_index % padded).astype(jnp.float32) * (2.0 * jnp.pi / padded)
    cosine = jnp.cos(phase)
    sine_table = jnp.sin(phase)
    weight = (
        jnp.where((freq_index == 0) | (freq_index == freq_count - 1), 1.0, 2.0).astype(jnp.float32)
        / padded
    )
    return (cosine, sine_table, cosine * weight, sine_table * weight)


def batched(matrix, vector):
    return jnp.einsum("fsc,fc->fs", matrix, vector, preferred_element_type=jnp.float32)


def transposed(matrix, vector):
    return jnp.einsum("fsc,fs->fc", matrix, vector, preferred_element_type=jnp.float32)


def with_rims(values):
    return padded_2(values, (("cell", 2),), COLS)


def penalty_margins(penalty):
    return with_rims(penalty)


def differences(extended, local_index, center):
    taken = [jnp.take(extended[0], local_index[direction], axis=1) for direction in range(4)]
    return jnp.stack(taken) - center[None]


def divergence(extended, local_index, linked, own):
    accumulated = jnp.zeros(own.shape[1:], jnp.float32)
    for direction in range(4):
        partner = direction ^ 1
        arriving = jnp.take(extended[direction], local_index[partner], axis=1)
        accumulated = accumulated + linked[partner] * arriving - linked[direction] * own[direction]
    return accumulated


def per_device(
    kernel, observed, start_model, start_multiplier, neighbours, tile_of_cell, tile_weight
):
    times_count = start_model.shape[0]
    freq_count = kernel.shape[1]
    cell_count = start_model.shape[1]
    cosine, sine_table, cos_weighted, sin_weighted = tables(times_count, freq_count)
    offset = lax.axis_index("cell") * cell_count
    own_cells = offset + lax.broadcasted_iota(jnp.int32, (1, cell_count), 1)
    linked = (neighbours != own_cells).astype(jnp.float32)
    local_index = neighbours - offset + COLS
    labels = lax.broadcasted_iota(jnp.int32, (tile_weight.shape[0], cell_count), 0)
    threshold = SHRINK_SCALE * jnp.sum(
        jnp.where(labels == tile_of_cell[None, :], tile_weight[:, None], 0.0), axis=0
    )

    def synthesis(out_real, out_imag):
        return exact_dot(cos_weighted.T, out_real) - exact_dot(sin_weighted.T, out_imag)

    def forward(series):
        real_part = exact_dot(cosine, series).astype(jnp.bfloat16)
        imag_part = (-exact_dot(sine_table, series)).astype(jnp.bfloat16)
        out_real = batched(kernel[0], real_part) - batched(kernel[1], imag_part)
        out_imag = batched(kernel[0], imag_part) + batched(kernel[1], real_part)
        return lax.psum(synthesis(out_real, out_imag), "cell")

    estimate = start_model
    multiplier = start_multiplier
    predicted = forward(estimate)
    model_jumps = differences(with_rims(estimate[None]), local_index, estimate)
    auxiliary = model_jumps
    for iteration in range(ITERS):
        penalty = model_jumps - auxiliary + multiplier
        misfit = predicted - observed
        back_real = exact_dot(cos_weighted, misfit).astype(jnp.bfloat16)
        back_imag = (-exact_dot(sin_weighted, misfit)).astype(jnp.bfloat16)
        adjoint_spec_real = transposed(kernel[0], back_real) + transposed(kernel[1], back_imag)
        adjoint_spec_imag = transposed(kernel[0], back_imag) - transposed(kernel[1], back_real)
        gradient = lax.psum(
            exact_dot(cosine.T, adjoint_spec_real) - exact_dot(sine_table.T, adjoint_spec_imag),
            "sensor",
        ) + divergence(penalty_margins(penalty), local_index, linked, penalty)
        response = forward(gradient)
        grad_jumps = differences(with_rims(gradient[None]), local_index, gradient)
        grad_square = jnp.sum(gradient * gradient)
        jump_square = jnp.sum(grad_jumps * grad_jumps)
        response_square = jnp.sum(response * response)
        grad_square, jump_square = lax.psum((grad_square, jump_square), "cell")
        response_square = lax.psum(response_square, "sensor")
        step_size = grad_square / (response_square + jump_square + TINY)
        estimate = estimate - step_size * gradient
        predicted = predicted - step_size * response
        model_jumps = model_jumps - step_size * grad_jumps
        shifted = model_jumps + multiplier
        auxiliary = jnp.sign(shifted) * jnp.maximum(jnp.abs(shifted) - threshold, 0.0)
        multiplier = shifted - auxiliary
    return (estimate, auxiliary, multiplier)


def solution(mesh):
    in_specs = (
        P(None, None, "sensor", "cell"),
        P(None, "sensor"),
        P(None, "cell"),
        P(None, None, "cell"),
        P(None, "cell"),
        P("cell"),
        P(),
    )
    out_specs = (P(None, "cell"), P(None, None, "cell"), P(None, None, "cell"))
    return jax.shard_map(
        per_device, mesh=mesh, in_specs=in_specs, out_specs=out_specs, check_vma=False
    )
```

profile of v0, /device:TPU:0, one launch (start us, length us, event | category | flops | bytes accessed | tf_op | source)
XLA Modules:
  0.0 284.5 jit_solution(4986496396985905231)
XLA Ops:
  8.6 2.2 fusion.36
  10.8 2.3 fusion.18
  15.6 38.9 %psum.77 = f32[64,64]{1,0:T(8,128)S(1)} all-reduce(f32[64,64]{1,0:T(8,128)S(1)} %convolution_subtract_fusion.4), channel_id=1, replica_groups=mesh['cell'=8,'sensor'=4] {'cell'}, use_global_device_ids=true, to_apply=%region_0.1 | all-reduce | flops 4096 | bytes 32768 | tf_op jit(solution)/shard_map/psum | solution.py:99
  61.5 2.0 fusion.34
  68.3 4.3 %collective-permute-done.1 = f32[1,64,128]{1,2,0:T(8,128)S(1)} collective-permute-done((f32[1,64,128]{1,2,0:T(8,128)S(1)}, f32[1,64,128]{1,2,0:T(8,128)S(1)}, u32[]{:S(2)}, u32[]{:S(2)}) %collective-permute-start.1) | collective-permute-done | bytes 32800 | tf_op jit(solution)/shard_map/ppermute | solution.py:22
  76.0 3.8 %collective-permute-start.2 = (f32[4,64,128]{2,1,0:T(8,128)S(1)}, f32[4,64,128]{2,1,0:T(8,128)S(1)}, u32[]{:S(2)}, u32[]{:S(2)}) collective-permute-start(f32[4,64,128]{2,1,0:T(8,128)S(1)} %get-tuple-element.26), channel_id=1, source_target_pairs={{0,4},{4,8},{8,12},{12,16},{16,20},{20,24},{24,28},{1,5},{5,9},{9,... | collective-permute-start | bytes 393224 | tf_op jit(solution)/shard_map/ppermute | solution.py:21
  82.3 4.4 %collective-permute-done.3 = f32[4,64,128]{2,1,0:T(8,128)S(1)} collective-permute-done((f32[4,64,128]{2,1,0:T(8,128)S(1)}, f32[4,64,128]{2,1,0:T(8,128)S(1)}, u32[]{:S(2)}, u32[]{:S(2)}) %collective-permute-start.3) | collective-permute-done | bytes 131104 | tf_op jit(solution)/shard_map/ppermute | solution.py:22
  90.6 2.9 %all-reduce.5.cloned.1.call-done = f32[64,256]{1,0:T(8,128)} async-done(((f32[64,256]{1,0:T(8,128)}), f32[64,256]{1,0:T(8,128)}) %all-reduce.5.cloned.1.call-update) | async-done | bytes 65552 | tf_op jit(solution)/shard_map/psum | solution.py:113
  95.3 2.4 fusion.28
  97.7 2.3 fusion.10
  100.4 2.3 fusion.8
  103.3 3.4 %collective-permute-start.4 = (f32[1,64,128]{2,1,0:T(8,128)S(1)}, f32[1,64,128]{2,1,0:T(8,128)S(1)}, u32[]{:S(2)}, u32[]{:S(2)}) collective-permute-start(f32[1,64,128]{2,1,0:T(8,128)S(1)} %get-tuple-element.32), channel_id=1, source_target_pairs={{0,4},{4,8},{8,12},{12,16},{16,20},{20,24},{24,28},{1,5},{5,9},{9,... | collective-permute-start | bytes 98312 | tf_op jit(solution)/shard_map/ppermute | solution.py:21
  109.0 3.5 %collective-permute-done.5 = f32[1,64,128]{2,1,0:T(8,128)S(1)} collective-permute-done((f32[1,64,128]{2,1,0:T(8,128)S(1)}, f32[1,64,128]{2,1,0:T(8,128)S(1)}, u32[]{:S(2)}, u32[]{:S(2)}) %collective-permute-start.5) | collective-permute-done | bytes 32800 | tf_op jit(solution)/shard_map/ppermute | solution.py:22
  116.6 36.9 %all-reduce.1 = (f32[64,64]{1,0:T(8,128)S(1)}, f32[]{:T(128)}, f32[]{:T(128)}) all-reduce(f32[64,64]{1,0:T(8,128)S(1)} %convolution_subtract_fusion.3, f32[]{:T(128)} %get-tuple-element.14, f32[]{:T(128)} %multiply_reduce_fusion.1), channel_id=1, replica_groups=mesh['cell'=8,'sensor'=4] {'cell'}, use_global_device_ids=true, to_apply=%region_4.6 | all-reduce | flops 4098 | bytes 32784 | tf_op jit(solution)/shard_map/psum | solution.py:99
  154.1 6.4 %psum.81 = f32[]{:T(128)} all-reduce(f32[]{:T(128)} %multiply_reduce_fusion.5), channel_id=1, replica_groups=mesh['cell'=8,'sensor'=4] {'sensor'}, use_global_device_ids=true, to_apply=%region_6.8 | all-reduce | flops 1 | bytes 8 | tf_op jit(solution)/shard_map/psum | solution.py:123
  175.9 4.1 %collective-permute-done.7 = f32[4,64,128]{2,1,0:T(8,128)S(1)} collective-permute-done((f32[4,64,128]{2,1,0:T(8,128)S(1)}, f32[4,64,128]{2,1,0:T(8,128)S(1)}, u32[]{:S(2)}, u32[]{:S(2)}) %collective-permute-start.7) | collective-permute-done | bytes 131104 | tf_op jit(solution)/shard_map/ppermute | solution.py:22
  183.8 23.1 %all-reduce.7.cloned.1.call-done = f32[64,256]{1,0:T(8,128)} async-done(((f32[64,256]{1,0:T(8,128)}), f32[64,256]{1,0:T(8,128)}) %all-reduce.7.cloned.1.call-update) | async-done | bytes 65552 | tf_op jit(solution)/shard_map/psum | solution.py:113
  208.8 2.4 fusion.20
  211.2 2.3 fusion.2
  213.8 2.3 fusion
  216.8 3.4 %collective-permute-start.8 = (f32[1,64,128]{2,1,0:T(8,128)S(1)}, f32[1,64,128]{2,1,0:T(8,128)S(1)}, u32[]{:S(2)}, u32[]{:S(2)}) collective-permute-start(f32[1,64,128]{2,1,0:T(8,128)S(1)} %get-tuple-element.30), channel_id=1, source_target_pairs={{0,4},{4,8},{8,12},{12,16},{16,20},{20,24},{24,28},{1,5},{5,9},{9,... | collective-permute-start | bytes 98312 | tf_op jit(solution)/shard_map/ppermute | solution.py:21
  222.3 3.7 %collective-permute-done.9 = f32[1,64,128]{2,1,0:T(8,128)S(1)} collective-permute-done((f32[1,64,128]{2,1,0:T(8,128)S(1)}, f32[1,64,128]{2,1,0:T(8,128)S(1)}, u32[]{:S(2)}, u32[]{:S(2)}) %collective-permute-start.9) | collective-permute-done | bytes 32800 | tf_op jit(solution)/shard_map/ppermute | solution.py:22
  230.1 36.9 %all-reduce = (f32[]{:T(128)}, f32[64,64]{1,0:T(8,128)S(1)}, f32[]{:T(128)}) all-reduce(f32[]{:T(128)} %get-tuple-element.12, f32[64,64]{1,0:T(8,128)S(1)} %convolution_subtract_fusion.2, f32[]{:T(128)} %multiply_reduce_fusion), channel_id=1, replica_groups=mesh['cell'=8,'sensor'=4] {'cell'}, use_global_device_ids=true, to_apply=%region_12.14 | all-reduce | flops 4098 | bytes 32784 | tf_op jit(solution)/shard_map/psum | solution.py:122
  267.6 6.4 %psum.86 = f32[]{:T(128)} all-reduce(f32[]{:T(128)} %multiply_reduce_fusion.4), channel_id=1, replica_groups=mesh['cell'=8,'sensor'=4] {'sensor'}, use_global_device_ids=true, to_apply=%region_15.17 | all-reduce | flops 1 | bytes 8 | tf_op jit(solution)/shard_map/psum | solution.py:123
  (179 shorter events, 63.4 us)
Async XLA Ops:
  7.2 6.0 %copy-start.2 = (f32[64,256]{1,0:T(8,128)S(1)}, f32[64,256]{1,0:T(8,128)}, u32[]{:S(2)}) copy-start(f32[64,256]{1,0:T(8,128)} %param.11) | copy-start | bytes 196612
  7.2 86.3 %all-reduce.5.cloned.1.call-start = ((), (), s32[]{:S(2)}) async-start(), calls=%async_computation | async-start | bytes 131072 | tf_op jit(solution)/shard_map/psum | solution.py:113
  7.2 6.3 %copy-start = (bf16[2,65,64,256]{3,2,1,0:T(8,128)(2,1)S(1)}, bf16[2,65,64,256]{3,2,1,0:T(8,128)(2,1)}, u32[]{:S(2)}) copy-start(bf16[2,65,64,256]{3,2,1,0:T(8,128)(2,1)} %param.9) | copy-start | bytes 12779524
  10.8 43.7 %copy-start.3 = (f32[64,64]{1,0:T(8,128)S(1)}, f32[64,64]{1,0:T(8,128)}, u32[]{:S(2)}) copy-start(f32[64,64]{1,0:T(8,128)} %param.10) | copy-start | bytes 49156
  57.3 10.4 %copy-start.4 = (s32[4,256]{1,0:T(4,128)S(1)}, s32[4,256]{1,0:T(4,128)}, u32[]{:S(2)}) copy-start(s32[4,256]{1,0:T(4,128)} %param.13) | copy-start | bytes 12292
  61.4 14.5 %copy-start.1 = (f32[4,64,256]{2,1,0:T(8,128)S(1)}, f32[4,64,256]{2,1,0:T(8,128)}, u32[]{:S(2)}) copy-start(f32[4,64,256]{2,1,0:T(8,128)} %param.12) | copy-start | bytes 786436
  61.4 19.6 %copy-start.5 = (s32[256]{0:T(256)S(1)}, s32[256]{0:T(256)}, u32[]{:S(2)}) copy-start(s32[256]{0:T(256)} %param.14) | copy-start | bytes 3076
  61.4 19.6 %copy-start.6 = (f32[64]{0:T(128)S(1)}, f32[64]{0:T(128)}, u32[]{:S(2)}) copy-start(f32[64]{0:T(128)} %param.15) | copy-start | bytes 772
  65.0 141.9 %all-reduce.7.cloned.1.call-start = ((), (), s32[]{:S(2)}) async-start(), calls=%async_computation.1 | async-start | bytes 131072 | tf_op jit(solution)/shard_map/psum | solution.py:113
  65.1 3.2 %collective-permute-start = (f32[1,64,128]{1,2,0:T(8,128)S(1)}, f32[1,64,128]{1,2,0:T(8,128)S(1)}, u32[]{:S(2)}, u32[]{:S(2)}) collective-permute-start(f32[1,64,128]{1,2,0:T(8,128)S(1)} %get-tuple-element.28), channel_id=1, source_target_pairs={{0,4},{4,8},{8,12},{12,16},{16,20},{20,24},{24,28},{1,5},{5,9},{9,... | collective-permute-start | bytes 98312 | tf_op jit(solution)/shard_map/ppermute | solution.py:21
  66.4 6.2 %collective-permute-start.1 = (f32[1,64,128]{1,2,0:T(8,128)S(1)}, f32[1,64,128]{1,2,0:T(8,128)S(1)}, u32[]{:S(2)}, u32[]{:S(2)}) collective-permute-start(f32[1,64,128]{1,2,0:T(8,128)S(1)} %get-tuple-element.29), channel_id=1, source_target_pairs={{4,0},{8,4},{12,8},{16,12},{20,16},{24,20},{28,24},{5,1},{9,5},{13... | collective-permute-start | bytes 98312 | tf_op jit(solution)/shard_map/ppermute | solution.py:22
  76.0 6.3 %collective-permute-start.2 = (f32[4,64,128]{2,1,0:T(8,128)S(1)}, f32[4,64,128]{2,1,0:T(8,128)S(1)}, u32[]{:S(2)}, u32[]{:S(2)}) collective-permute-start(f32[4,64,128]{2,1,0:T(8,128)S(1)} %get-tuple-element.26), channel_id=1, source_target_pairs={{0,4},{4,8},{8,12},{12,16},{16,20},{20,24},{24,28},{1,5},{5,9},{9,... | collective-permute-start | bytes 393224 | tf_op jit(solution)/shard_map/ppermute | solution.py:21
  79.8 6.9 %collective-permute-start.3 = (f32[4,64,128]{2,1,0:T(8,128)S(1)}, f32[4,64,128]{2,1,0:T(8,128)S(1)}, u32[]{:S(2)}, u32[]{:S(2)}) collective-permute-start(f32[4,64,128]{2,1,0:T(8,128)S(1)} %get-tuple-element.27), channel_id=1, source_target_pairs={{4,0},{8,4},{12,8},{16,12},{20,16},{24,20},{28,24},{5,1},{9,5},{13... | collective-permute-start | bytes 393224 | tf_op jit(solution)/shard_map/ppermute | solution.py:22
  86.7 16.0 %slice-start = ((s8[4259840]{0:T(1024)(128)(4,1)}), s8[65536]{0:T(1024)(128)(4,1)S(1)}, s32[]{:S(2)}) async-start(s8[4259840]{0:T(1024)(128)(4,1)} %bitcast.363), calls=%async_computation.2 | async-start | bytes 131072
  94.9 7.7 %slice-start.1 = ((s8[4259840]{0:T(1024)(128)(4,1)}), s8[4194304]{0:T(1024)(128)(4,1)S(1)}, s32[]{:S(2)}) async-start(s8[4259840]{0:T(1024)(128)(4,1)} %bitcast.363), calls=%async_computation.3 | async-start | bytes 8388608
  103.3 5.7 %collective-permute-start.4 = (f32[1,64,128]{2,1,0:T(8,128)S(1)}, f32[1,64,128]{2,1,0:T(8,128)S(1)}, u32[]{:S(2)}, u32[]{:S(2)}) collective-permute-start(f32[1,64,128]{2,1,0:T(8,128)S(1)} %get-tuple-element.32), channel_id=1, source_target_pairs={{0,4},{4,8},{8,12},{12,16},{16,20},{20,24},{24,28},{1,5},{5,9},{9,... | collective-permute-start | bytes 98312 | tf_op jit(solution)/shard_map/ppermute | solution.py:21
  106.7 5.8 %collective-permute-start.5 = (f32[1,64,128]{2,1,0:T(8,128)S(1)}, f32[1,64,128]{2,1,0:T(8,128)S(1)}, u32[]{:S(2)}, u32[]{:S(2)}) collective-permute-start(f32[1,64,128]{2,1,0:T(8,128)S(1)} %get-tuple-element.33), channel_id=1, source_target_pairs={{4,0},{8,4},{12,8},{16,12},{20,16},{24,20},{28,24},{5,1},{9,5},{13... | collective-permute-start | bytes 98312 | tf_op jit(solution)/shard_map/ppermute | solution.py:22
  171.6 4.2 %collective-permute-start.6 = (f32[4,64,128]{2,1,0:T(8,128)S(1)}, f32[4,64,128]{2,1,0:T(8,128)S(1)}, u32[]{:S(2)}, u32[]{:S(2)}) collective-permute-start(f32[4,64,128]{2,1,0:T(8,128)S(1)} %get-tuple-element.24), channel_id=1, source_target_pairs={{0,4},{4,8},{8,12},{12,16},{16,20},{20,24},{24,28},{1,5},{5,9},{9,... | collective-permute-start | bytes 393224 | tf_op jit(solution)/shard_map/ppermute | solution.py:21
  172.9 7.0 %collective-permute-start.7 = (f32[4,64,128]{2,1,0:T(8,128)S(1)}, f32[4,64,128]{2,1,0:T(8,128)S(1)}, u32[]{:S(2)}, u32[]{:S(2)}) collective-permute-start(f32[4,64,128]{2,1,0:T(8,128)S(1)} %get-tuple-element.25), channel_id=1, source_target_pairs={{4,0},{8,4},{12,8},{16,12},{20,16},{24,20},{28,24},{5,1},{9,5},{13... | collective-permute-start | bytes 393224 | tf_op jit(solution)/shard_map/ppermute | solution.py:22
  179.9 36.2 %slice-start.2 = ((s8[4259840]{0:T(1024)(128)(4,1)}), s8[65536]{0:T(1024)(128)(4,1)S(1)}, s32[]{:S(2)}) async-start(s8[4259840]{0:T(1024)(128)(4,1)} %bitcast.365), calls=%async_computation.4 | async-start | bytes 131072
  208.4 7.7 %slice-start.3 = ((s8[4259840]{0:T(1024)(128)(4,1)}), s8[4194304]{0:T(1024)(128)(4,1)S(1)}, s32[]{:S(2)}) async-start(s8[4259840]{0:T(1024)(128)(4,1)} %bitcast.365), calls=%async_computation.5 | async-start | bytes 8388608
  216.8 5.5 %collective-permute-start.8 = (f32[1,64,128]{2,1,0:T(8,128)S(1)}, f32[1,64,128]{2,1,0:T(8,128)S(1)}, u32[]{:S(2)}, u32[]{:S(2)}) collective-permute-start(f32[1,64,128]{2,1,0:T(8,128)S(1)} %get-tuple-element.30), channel_id=1, source_target_pairs={{0,4},{4,8},{8,12},{12,16},{16,20},{20,24},{24,28},{1,5},{5,9},{9,... | collective-permute-start | bytes 98312 | tf_op jit(solution)/shard_map/ppermute | solution.py:21
  220.2 5.8 %collective-permute-start.9 = (f32[1,64,128]{2,1,0:T(8,128)S(1)}, f32[1,64,128]{2,1,0:T(8,128)S(1)}, u32[]{:S(2)}, u32[]{:S(2)}) collective-permute-start(f32[1,64,128]{2,1,0:T(8,128)S(1)} %get-tuple-element.31), channel_id=1, source_target_pairs={{4,0},{8,4},{12,8},{16,12},{20,16},{24,20},{28,24},{5,1},{9,5},{13... | collective-permute-start | bytes 98312 | tf_op jit(solution)/shard_map/ppermute | solution.py:22
Sparse Core Ops, SparseCore 0:
  65.1 28.2 all-reduce.4
  175.8 31.0 all-reduce.6
where the time goes:
time: 286 us; the launch traced here: 285 us
  blocking collectives  125 us (44%)
  waiting for transfers between devices  47.6 us (17%)
  matrix products  46.9 us (16%)
  starting transfers between devices  19.8 us (7%)
  between operations  18.8 us (7%)
  local copies, waits for them, and re-layouts  18.1 us (6%)
  other arithmetic  7.93 us (3%)
    psum x2, blocking collectives, forward(): return lax.psum(synthesis(out_real, out_imag), 'cell')  75.7 us
    psum x1, blocking collectives, per_device(): grad_square, jump_square = lax.psum((grad_square, jump_square), 'cell')  36.9 us
    psum x2, waiting for transfers between devices, per_device(): lax.psum(exact_dot(cosine.T, adjoint_spec_real) - exact_dot(sine_table.T,...  26 us
    dot_general x12, matrix products, batched(): jnp.einsum('fsc,fc->fs', matrix, vector, preferred_element_type=jnp.float32)  21.1 us
    ppermute x5, waiting for transfers between devices, padded_2(): after = lax.ppermute(leading, axis, down)  20 us
    dot_general x8, matrix products, transposed(): jnp.einsum('fsc,fs->fc', matrix, vector, preferred_element_type=jnp.float32)  16 us
    ppermute x5, starting transfers between devices, padded_2(): before = lax.ppermute(last, axis, up)  13.1 us
    psum x2, blocking collectives, per_device(): response_square = lax.psum(response_square, 'sensor')  12.8 us
  transfers between devices with their start and end apart: 12, of which 10 were waited for; matrix products, arithmetic and copies ran while one was open for 5% of the time, Pallas kernels for 0%

commit v1 on v0

v1 whole, which is shorter than its diff:
```python
import functools

import jax
import jax.numpy as jnp
import numpy as np
from jax import lax
from jax.experimental import pallas as pl
from jax.experimental.pallas import tpu as pltpu
from jax.sharding import PartitionSpec as P

COLS = 128
LANES = 128
GROUP = 8
SHRINK_SCALE = 0.4
TINY = 1e-06
VMEM = pltpu.VMEM


def tables(times, freqs):
    padded = 2 * times
    groups = -(-freqs // GROUP)
    plain = np.zeros((16 * groups, times), np.float64)
    weighted = np.zeros((16 * groups, times), np.float64)
    for f in range(freqs):
        phase = 2.0 * np.pi * ((f * np.arange(times)) % padded) / padded
        weight = (1.0 if f in (0, freqs - 1) else 2.0) / padded
        row = 16 * (f // GROUP) + f % GROUP
        plain[row], plain[row + GROUP] = np.cos(phase), -np.sin(phase)
        weighted[row], weighted[row + GROUP] = weight * np.cos(phase), -weight * np.sin(phase)
    return plain.astype(np.float32), weighted.astype(np.float32)


def exact(left, right):
    return jnp.dot(left, right, precision=lax.Precision.HIGHEST, preferred_element_type=jnp.float32)


def turned(rows):
    return jnp.concatenate([-rows[GROUP:], rows[:GROUP]], axis=0)


def dot_nt(left, right):
    return lax.dot_general(left, right, (((1,), (1,)), ((), ())), preferred_element_type=jnp.float32)


def dot_nn(left, right):
    return jnp.dot(left, right, preferred_element_type=jnp.float32)


def slab(kernel_ref, part, group):
    freqs, sensors, cells = kernel_ref.shape[1:]
    count = min(GROUP, freqs - group * GROUP)
    block = kernel_ref[part, group * GROUP : group * GROUP + count]
    return block.reshape(count * sensors, cells)


def own_block(width, sensors):
    row = lax.broadcasted_iota(jnp.int32, (16, width), 0) % GROUP
    lane = lax.broadcasted_iota(jnp.int32, (16, width), 1) // sensors
    return row == lane


def fold(wide):
    total = functools.reduce(
        lambda a, b: a + b, [wide[:, i : i + LANES] for i in range(0, wide.shape[1], LANES)]
    )
    return total + pltpu.roll(total, LANES // 2, 1)


def forward(field, kernel_ref, plain, weighted_t):
    freqs, sensors = kernel_ref.shape[1:3]
    times = field.shape[0]
    spectra = exact(plain, field)
    rows = []
    for group in range(plain.shape[0] // 16):
        part = spectra[16 * group : 16 * group + 16]
        re_slab, im_slab = slab(kernel_ref, 0, group), slab(kernel_ref, 1, group)
        out = dot_nt(part.astype(jnp.bfloat16), re_slab) + dot_nt(turned(part).astype(jnp.bfloat16), im_slab)
        width = out.shape[1]
        out = jnp.where(own_block(width, sensors), out, 0.0)
        if width < LANES:
            out = jnp.concatenate([out, jnp.zeros((16, LANES - width), jnp.float32)], axis=1)
        rows.append(fold(out))
    series = exact(weighted_t, jnp.concatenate(rows, axis=0))
    left = lax.broadcasted_iota(jnp.int32, (times // 2, LANES), 1) < sensors
    return jnp.where(left, series[: times // 2], series[times // 2 :])


def unpacked(packed, sensors):
    other = pltpu.roll(packed, sensors, 1)
    left = lax.broadcasted_iota(jnp.int32, packed.shape, 1) < sensors
    return jnp.concatenate([jnp.where(left, packed, other), jnp.where(left, other, packed)], axis=0)


def adjoint(residual, kernel_ref, plain_t, weighted, halves):
    freqs, sensors, cells = kernel_ref.shape[1:]
    spectra = exact(weighted, residual)
    rows = []
    for group in range(weighted.shape[0] // 16):
        part = spectra[16 * group : 16 * group + 16]
        count = min(GROUP, freqs - group * GROUP)
        width = count * sensors
        re_slab, im_slab = slab(kernel_ref, 0, group), slab(kernel_ref, 1, group)
        wide = jnp.concatenate([part] * (-(-width // LANES)), axis=1)[:, :width]
        wide = jnp.where(own_block(width, sensors), wide, 0.0)
        total = None
        for _ in range(halves):
            re_left = wide.astype(jnp.bfloat16)
            rounded = re_left.astype(jnp.float32)
            out = dot_nn(re_left, re_slab) - dot_nn(turned(rounded).astype(jnp.bfloat16), im_slab)
            total = out if total is None else total + out
            wide = wide - rounded
        rows.append(total)
    return exact(plain_t, jnp.concatenate(rows, axis=0))


def strip(array, row):
    return array[..., row * COLS : (row + 1) * COLS]


def jumps(field, above, below, linked):
    count = field.shape[1] // COLS
    out = []
    for direction in range(4):
        strips = []
        for row in range(count):
            here = strip(field, row)
            if direction == 0:
                there = pltpu.roll(here, COLS - 1, 1)
            elif direction == 1:
                there = pltpu.roll(here, 1, 1)
            elif direction == 2:
                there = above if row == 0 else strip(field, row - 1)
            else:
                there = below if row == count - 1 else strip(field, row + 1)
            strips.append(strip(linked[direction : direction + 1], row) * (there - here))
        out.append(strips)
    return out


def gathered_jumps(values, above, below, linked):
    count = len(values[0])
    out = []
    for row in range(count):
        arriving = (
            pltpu.roll(values[1][row], COLS - 1, 1),
            pltpu.roll(values[0][row], 1, 1),
            above if row == 0 else values[3][row - 1],
            below if row == count - 1 else values[2][row + 1],
        )
        total = None
        for direction in range(4):
            term = strip(linked[direction : direction + 1], row) * (arriving[direction] - values[direction][row])
            total = term if total is None else total + term
        out.append(total)
    return jnp.concatenate(out, axis=1)


def shrunk(shifted, threshold):
    return shifted - jnp.clip(shifted, -threshold, threshold)


def tree_sum(parts):
    parts = list(parts)
    while len(parts) > 1:
        parts = [parts[i] + parts[i + 1] if i + 1 < len(parts) else parts[i] for i in range(0, len(parts), 2)]
    return parts[0]


def square_sum(array):
    return jnp.sum(array * array)


def block_of(scalar, rows=8):
    return jnp.full((rows, LANES), scalar, jnp.float32)


def call(body, out_shapes, *operands, flops=0):
    single = isinstance(out_shapes, tuple)
    shapes = [out_shapes] if single else list(out_shapes)
    out = pl.pallas_call(
        body,
        out_shape=[jax.ShapeDtypeStruct(s, jnp.float32) for s in shapes],
        in_specs=[pl.BlockSpec(memory_space=VMEM)] * len(operands),
        out_specs=[pl.BlockSpec(memory_space=VMEM)] * len(shapes),
        compiler_params=pltpu.CompilerParams(vmem_limit_bytes=24 * 2**20),
    )(*operands)
    return out[0] if single else out


def forward_body(field, kernel, plain, weighted_t, out):
    out[...] = forward(field[...], kernel, plain[...], weighted_t[...])


def first_adjoint_body(parts_count, *refs):
    parts, (observed, kernel, plain_t, weighted, out) = refs[:parts_count], refs[parts_count:]
    predicted = unpacked(tree_sum([p[...] for p in parts]), kernel.shape[2])
    out[...] = adjoint(predicted - observed[...], kernel, plain_t[...], weighted[...], 1)


def first_gradient_body(parts_count, *refs):
    parts, (start_multiplier, above, below, linked, adjoint_out, gradient) = refs[:parts_count], refs[parts_count:]
    times, cells = adjoint_out.shape
    total = tree_sum([p[...] for p in parts])
    values = [[strip(start_multiplier[k], r) for r in range(cells // COLS)] for k in range(4)]
    back = gathered_jumps(values, above[times : 2 * times], below[times : 2 * times], linked[...])
    adjoint_out[...] = total
    gradient[...] = total + back


def norms_body(gradient, above, below, linked, out):
    field = gradient[...]
    squares = [square_sum(s) for strips in jumps(field, above[...], below[...], linked[...]) for s in strips]
    out[0:8, :] = block_of(square_sum(field))
    out[8:16, :] = block_of(tree_sum(squares))


def second_adjoint_body(parts_count, norms_count, *refs):
    parts, norms = refs[:parts_count], refs[parts_count : parts_count + norms_count]
    kernel, plain_t, weighted, out = refs[parts_count + norms_count :]
    times = plain_t.shape[0]
    packed = tree_sum([p[...] for p in parts])
    out[:times, :] = adjoint(unpacked(packed, kernel.shape[2]), kernel, plain_t[...], weighted[...], 2)
    squares = tree_sum([n[...] for n in norms])
    out[times : times + 8, :LANES] = squares[:8]
    out[times : times + 8, LANES : 2 * LANES] = squares[8:]
    out[times + 8 : times + 16, :LANES] = block_of(square_sum(packed))
    out[times + 8 : times + 16, LANES : 2 * LANES] = jnp.zeros((8, LANES), jnp.float32)


def second_gradient_body(parts_count, *refs):
    parts = refs[:parts_count]
    (adjoint_in, gradient_in, model, start_multiplier, threshold, above, below, grad_above, grad_below, linked_ref,
     model_out, jumps_out, multiplier_out, gradient_out) = refs[parts_count:]
    times, cells = model.shape
    total = tree_sum([p[...] for p in parts])
    grad_square, jump_square = total[times, 0], total[times, LANES]
    response_square = total[times + 8, 0]
    step = grad_square / (response_square + jump_square + TINY)
    linked = linked_ref[...]
    field, gradient = model[...], gradient_in[...]
    rows = cells // COLS
    field_jumps = jumps(field, above[:times], below[:times], linked)
    grad_jumps = jumps(gradient, grad_above[...], grad_below[...], linked)

    def advance(model_jumps, old_multiplier, limit):
        shifted = model_jumps + old_multiplier
        auxiliary = shrunk(shifted, limit)
        multiplier = shifted - auxiliary
        return multiplier, model_jumps - auxiliary + multiplier

    penalties, new_jumps = [], []
    for k in range(4):
        penalties.append([])
        new_jumps.append([])
        for r in range(rows):
            new = field_jumps[k][r] - step * grad_jumps[k][r]
            multiplier, penalty = advance(new, strip(start_multiplier[k], r), strip(threshold[0:1], r))
            jumps_out[k, :, r * COLS : (r + 1) * COLS] = new
            multiplier_out[k, :, r * COLS : (r + 1) * COLS] = multiplier
            penalties[k].append(penalty)
            new_jumps[k].append(new)
    _, beside_above = advance(-new_jumps[2][0], above[times : 2 * times], above[2 * times : 2 * times + 1])
    _, beside_below = advance(-new_jumps[3][-1], below[times : 2 * times], below[2 * times : 2 * times + 1])
    back = gathered_jumps(penalties, beside_above, beside_below, linked)
    model_out[...] = field - step * gradient
    gradient_out[...] = adjoint_in[...] - step * total[:times] + back


def response_body(parts_count, *refs):
    parts, out = refs[:parts_count], refs[parts_count]
    out[...] = block_of(square_sum(tree_sum([p[...] for p in parts])))


def finish_body(norms, gradient_in, model, model_jumps, multiplier, threshold, above, below, linked, *outs):
    estimate_out, auxiliary_out, multiplier_out = outs
    step = norms[0, 0] / (norms[16, 0] + norms[8, 0] + TINY)
    gradient = gradient_in[...]
    estimate_out[...] = model[...] - step * gradient
    grad_jumps = jumps(gradient, above[...], below[...], linked[...])
    for k in range(4):
        for r in range(gradient.shape[1] // COLS):
            at = slice(r * COLS, (r + 1) * COLS)
            shifted = model_jumps[k, :, at] - step * grad_jumps[k][r] + multiplier[k, :, at]
            auxiliary = shrunk(shifted, threshold[0:1, at])
            auxiliary_out[k, :, at] = auxiliary
            multiplier_out[k, :, at] = shifted - auxiliary


def parts_of(array, axis):
    count = lax.axis_size(axis)
    if count & (count - 1):
        return list(lax.all_gather(array, axis))
    return [array] + [lax.ppermute(array, axis, [(i, i ^ k) for i in range(count)]) for k in range(1, count)]


def parts_by_all_to_all(array, axis):
    count = lax.axis_size(axis)
    sent = jnp.broadcast_to(array[None], (count,) + array.shape)
    return list(lax.all_to_all(sent, axis, 0, 0))


def rows_beside(last, first, axis):
    count = lax.axis_size(axis)
    down = [(i, i + 1) for i in range(count - 1)]
    up = [(j, i) for i, j in down]
    return lax.ppermute(last, axis, down), lax.ppermute(first, axis, up)


def cell_shares(array):
    cells, sensors = lax.axis_size("cell"), lax.axis_size("sensor")
    if cells % sensors:
        return [lax.psum(array, "cell") / sensors]
    each = cells // sensors
    return [
        lax.ppermute(
            array,
            ("cell", "sensor"),
            [(((c + s * each + j) % cells) * sensors + s, c * sensors + s) for c in range(cells) for s in range(sensors)],
        )
        for j in range(each)
    ]


def per_device(kernel, observed, start_model, start_multiplier, neighbours, tile_of_cell, tile_weight):
    times, cells = start_model.shape
    freqs, sensors = kernel.shape[1:3]
    plain, weighted = tables(times, freqs)
    plain_t, weighted_t = jnp.asarray(plain.T.copy()), jnp.asarray(weighted.T.copy())
    plain, weighted = jnp.asarray(plain), jnp.asarray(weighted)
    cell_count, sensor_count = lax.axis_size("cell"), lax.axis_size("sensor")

    own = lax.axis_index("cell") * cells + lax.broadcasted_iota(jnp.int32, (1, cells), 1)
    linked = (neighbours != own).astype(jnp.float32)
    labels = lax.broadcasted_iota(jnp.int32, (tile_weight.shape[0], cells), 0)
    threshold = SHRINK_SCALE * jnp.sum(
        jnp.where(labels == tile_of_cell[None, :], tile_weight[:, None], 0.0), axis=0, keepdims=True
    )
    threshold = jnp.broadcast_to(threshold, (8, cells))
    observed_twice = jnp.concatenate([observed, observed], axis=1)
    last, first = slice(cells - COLS, cells), slice(0, COLS)
    above, below = rows_beside(
        jnp.concatenate([start_model[:, last], start_multiplier[3][:, last], threshold[:, last]]),
        jnp.concatenate([start_model[:, first], start_multiplier[2][:, first], threshold[:, first]]),
        "cell",
    )

    packed = (times // 2, 2 * sensors)
    field = (times, cells)
    wide = (4, times, cells)

    def forward_of(series):
        return parts_by_all_to_all(call(forward_body, packed, series, kernel, plain, weighted_t), "cell")

    parts = forward_of(start_model)
    back = call(
        functools.partial(first_adjoint_body, len(parts)), field, *parts, observed_twice, kernel, plain_t, weighted
    )
    parts = parts_of(back, "sensor")
    adjoint_one, gradient = call(
        functools.partial(first_gradient_body, len(parts)), [field, field],
        *parts, start_multiplier, above, below, linked,
    )
    grad_above, grad_below = rows_beside(gradient[:, last], gradient[:, first], "cell")
    parts = forward_of(gradient)
    norms = cell_shares(call(norms_body, (16, LANES), gradient, grad_above, grad_below, linked))
    back = call(
        functools.partial(second_adjoint_body, len(parts), len(norms)), (times + 16, cells),
        *parts, *norms, kernel, plain_t, weighted,
    )
    parts = parts_of(back, "sensor")
    model, model_jumps, multiplier, gradient_two = call(
        functools.partial(second_gradient_body, len(parts)), [field, wide, wide, field],
        *parts, adjoint_one, gradient, start_model, start_multiplier, threshold, above, below, grad_above, grad_below,
        linked,
    )
    grad_above, grad_below = rows_beside(gradient_two[:, last], gradient_two[:, first], "cell")
    parts = forward_of(gradient_two)
    norms = call(norms_body, (16, LANES), gradient_two, grad_above, grad_below, linked)
    response_square = call(functools.partial(response_body, len(parts)), (8, LANES), *parts)
    sums = lax.psum(
        jnp.concatenate([norms[:, 0] / sensor_count, response_square[:, 0] / cell_count]), ("cell", "sensor")
    )
    sums = jnp.broadcast_to(sums[:, None], (24, LANES))
    return tuple(
        call(
            finish_body, [field, wide, wide],
            sums, gradient_two, model, model_jumps, multiplier, threshold, grad_above, grad_below, linked,
        )
    )


def solution(mesh):
    in_specs = (
        P(None, None, "sensor", "cell"),
        P(None, "sensor"),
        P(None, "cell"),
        P(None, None, "cell"),
        P(None, "cell"),
        P("cell"),
        P(),
    )
    out_specs = (P(None, "cell"), P(None, None, "cell"), P(None, None, "cell"))
    return jax.shard_map(
        per_device, mesh=mesh, in_specs=in_specs, out_specs=out_specs, check_vma=False
    )
```

time: 286 us -> 126 us (0.44)
  blocking collectives: 125 us -> 42.4 us
  matrix products: 46.9 us -> 0 us
  waiting for transfers between devices: 47.6 us -> 13.3 us
  starting transfers between devices: 19.8 us -> 46.8 us
  between operations: 18.8 us -> 1.06 us
  Pallas kernels: 0 us -> 10.2 us
  other arithmetic: 7.93 us -> 0.51 us
  local copies, waits for them, and re-layouts: 18.1 us -> 11.4 us
    psum x5 -> x1, blocking collectives: 125 us -> 42.4 us  [per_device(): lax.psum(jnp.concatenate([norms[:, 0] / sensor_count, response_square[:,...]
    dot_general x40 -> x0, matrix products: 46.9 us -> none  [the longest x12 21.1 us: batched(): jnp.einsum('fsc,fc->fs', matrix, vector, preferred_element_type=jnp.float32)]
    psum x2 -> x0, waiting for transfers between devices: 26 us -> none  [per_device(): lax.psum(exact_dot(cosine.T, adjoint_spec_real) - exact_dot(sine_table.T,...]
    all_to_all x0 -> x3, starting transfers between devices: none -> 17.5 us  [parts_by_all_to_all(): return list(lax.all_to_all(sent, axis, 0, 0))]
    gather x40 -> x0, local copies, waits for them, and re-layouts: 16.2 us -> none  [the longest x24 9.67 us: differences(): jnp.take(extended[0], local_index[direction], axis=1)]
    pallas_call x0 -> x11, Pallas kernels: none -> 10.2 us  [call(): pl.pallas_call(body, out_shape=[jax.ShapeDtypeStruct(s, jnp.float32) for...]
    ppermute x10 -> x14, waiting for transfers between devices: 21.6 us -> 11.5 us  [the longest x6 7.66 us: parts_of(): lax.ppermute(array, axis, [(i, i ^ k) for i in range(count)])]
    ppermute x10 -> x14, starting transfers between devices: 19.8 us -> 29.3 us  [the longest x6 16.9 us: rows_beside(): return (lax.ppermute(last, axis, down), lax.ppermute(first, axis, up))]
  transfers between devices with their start and end apart: 12 -> 17, of which waited for: 10 -> 9; matrix products, arithmetic and copies ran while one was open for 5% -> 0% of each run, Pallas kernels for 0% -> 1%
where the time goes in v1:
time: 126 us
  starting transfers between devices  46.8 us (37%)
  blocking collectives  42.4 us (34%)
  waiting for transfers between devices  13.3 us (11%)
  local copies, waits for them, and re-layouts  11.4 us (9%)
  Pallas kernels  10.2 us (8%)
    psum x1, blocking collectives, per_device(): lax.psum(jnp.concatenate([norms[:, 0] / sensor_count, response_square[:,...  42.4 us
    all_to_all x3, starting transfers between devices, parts_by_all_to_all(): return list(lax.all_to_all(sent, axis, 0, 0))  17.5 us
    ppermute x6, starting transfers between devices, rows_beside(): return (lax.ppermute(last, axis, down), lax.ppermute(first, axis, up))  16.9 us
    pallas_call x11, Pallas kernels, call(): pl.pallas_call(body, out_shape=[jax.ShapeDtypeStruct(s, jnp.float32) for...  10.2 us
    unnamed x36, local copies, waits for them, and re-layouts  9.23 us
    ppermute x6, waiting for transfers between devices, parts_of(): lax.ppermute(array, axis, [(i, i ^ k) for i in range(count)])  7.66 us
    ppermute x2, starting transfers between devices, cell_shares(): lax.ppermute(array, ('cell', 'sensor'), [((c + s * each + j) % cells * se...  6.27 us
    ppermute x6, starting transfers between devices, parts_of(): lax.ppermute(array, axis, [(i, i ^ k) for i in range(count)])  6.1 us
  transfers between devices with their start and end apart: 17, of which 9 were waited for; matrix products, arithmetic and copies ran while one was open for 0% of the time, Pallas kernels for 1%

profile of v1, /device:TPU:0, one launch (start us, length us, event | category | flops | bytes accessed | tf_op | source)
XLA Modules:
  0.0 125.6 jit_solution(3335172860654363965)
XLA Ops:
  0.6 2.2 %copy-done = bf16[2,65,64,256]{3,2,1,0:T(8,128)(2,1)S(1)} copy-done((bf16[2,65,64,256]{3,2,1,0:T(8,128)(2,1)S(1)}, bf16[2,65,64,256]{3,2,1,0:T(8,128)(2,1)}, u32[]{:S(2)}) %copy-start) | copy-done | bytes 4259864
  5.5 1.7 %shard_map.130 = f32[32,128]{1,0:T(8,128)S(1)} custom-call(f32[64,256]{1,0:T(8,128)S(1)} %copy-done.10, bf16[2,65,64,256]{3,2,1,0:T(8,128)(2,1)S(1)} %copy-done, f32[144,64]{1,0:T(8,128)S(1)} %copy-done.6, f32[64,144]{1,0:T(8,128)S(1)} %copy-done.8), custom_call_target="tpu_custom_call" | custom-call | tf_op jit(solution)/shard_map/pallas_call | solution.py:180
  7.9 7.3 %all-to-all-start = ((f32[8,32,128]{2,1,0:T(8,128)}), f32[8,32,128]{2,1,0:T(8,128)S(1)}, u32[]{:S(2)}, u32[]{:S(2)}) async-start(f32[8,32,128]{2,1,0:T(8,128)} %broadcast_in_dim.26), calls=%async_computation | async-start | bytes 262144 | tf_op jit(solution)/shard_map/all_to_all | solution.py:299
  15.4 3.9 %collective-permute-start.3 = (f32[136,128]{1,0:T(8,128)S(1)}, f32[136,128]{1,0:T(8,128)S(1)}, u32[]{:S(2)}, u32[]{:S(2)}) collective-permute-start(f32[136,128]{1,0:T(8,128)S(1)} %pad_maximum_fusion), channel_id=1, source_target_pairs={{0,4},{4,8},{8,12},{12,16},{16,20},{20,24},{24,28},{1,5},{5,9},{9,... | collective-permute-start | bytes 208904 | tf_op jit(solution)/shard_map/ppermute | solution.py:306
  20.8 1.8 %all-to-all-done = f32[8,32,128]{2,1,0:T(8,128)S(1)} async-done(((f32[8,32,128]{2,1,0:T(8,128)}), f32[8,32,128]{2,1,0:T(8,128)S(1)}, u32[]{:S(2)}, u32[]{:S(2)}) %all-to-all-start) | async-done | bytes 131104 | tf_op jit(solution)/shard_map/all_to_all | solution.py:299
  22.6 2.2 %copy-done.1 = bf16[2,65,64,256]{3,2,1,0:T(8,128)(2,1)S(1)} copy-done((bf16[2,65,64,256]{3,2,1,0:T(8,128)(2,1)S(1)}, bf16[2,65,64,256]{3,2,1,0:T(8,128)(2,1)}, u32[]{:S(2)}) %copy-start.1) | copy-done | bytes 4259864
  26.1 1.6 %collective-permute-start.1 = (f32[64,256]{1,0:T(8,128)S(1)}, f32[64,256]{1,0:T(8,128)S(1)}, u32[]{:S(2)}, u32[]{:S(2)}) collective-permute-start(f32[64,256]{1,0:T(8,128)S(1)} %shard_map.131.refs_0_), channel_id=1, source_target_pairs={{0,2},{1,3},{2,0},{3,1},{4,6},{5,7},{6,4},{7,5},{8,10},{9,11},{10,... | collective-permute-start | bytes 196616 | tf_op jit(solution)/shard_map/ppermute | solution.py:293
  28.0 2.5 %collective-permute-done.2.refs_3_ = f32[64,256]{1,0:T(8,128)S(1)} collective-permute-done((f32[64,256]{1,0:T(8,128)S(1)}, f32[64,256]{1,0:T(8,128)S(1)}, u32[]{:S(2)}, u32[]{:S(2)}) %collective-permute-start.2) | collective-permute-done | bytes 65568 | tf_op jit(solution)/shard_map/ppermute | solution.py:293
  30.4 1.5 %collective-permute-done.1.refs_2_ = f32[64,256]{1,0:T(8,128)S(1)} collective-permute-done((f32[64,256]{1,0:T(8,128)S(1)}, f32[64,256]{1,0:T(8,128)S(1)}, u32[]{:S(2)}, u32[]{:S(2)}) %collective-permute-start.1) | collective-permute-done | bytes 65568 | tf_op jit(solution)/shard_map/ppermute | solution.py:293
  32.0 1.7 %shard_map.133 = f32[32,128]{1,0:T(8,128)S(1)} custom-call(f32[64,256]{1,0:T(8,128)S(1)} %get-tuple-element.9.field.gradient.refs_5_, bf16[2,65,64,256]{3,2,1,0:T(8,128)(2,1)S(1)} %copy-done.2, f32[144,64]{1,0:T(8,128)S(1)} %copy-done.7, f32[64,144]{1,0:T(8,128)S(1)} %copy-done.9), custom_call_target="tpu_custom_call" | custom-call | tf_op jit(solution)/shard_map/pallas_call | solution.py:180
  34.5 4.9 %all-to-all-start.1 = ((f32[8,32,128]{2,1,0:T(8,128)}), f32[8,32,128]{2,1,0:T(8,128)S(1)}, u32[]{:S(2)}, u32[]{:S(2)}) async-start(f32[8,32,128]{2,1,0:T(8,128)} %broadcast_in_dim.53), calls=%async_computation.1 | async-start | bytes 262144 | tf_op jit(solution)/shard_map/all_to_all | solution.py:299
  40.6 4.6 %collective-permute-start.5 = (f32[64,128]{1,0:T(8,128)S(1)}, f32[64,128]{1,0:T(8,128)S(1)}, u32[]{:S(2)}, u32[]{:S(2)}) collective-permute-start(f32[64,128]{1,0:T(8,128)S(1)} %get-tuple-element.44), channel_id=1, source_target_pairs={{0,4},{4,8},{8,12},{12,16},{16,20},{20,24},{24,28},{1,5},{5,9},{9,... | collective-permute-start | bytes 98312 | tf_op jit(solution)/shard_map/ppermute | solution.py:306
  45.4 1.4 %collective-permute-done.5.above.refs_11_ = f32[64,128]{1,0:T(8,128)S(1)} collective-permute-done((f32[64,128]{1,0:T(8,128)S(1)}, f32[64,128]{1,0:T(8,128)S(1)}, u32[]{:S(2)}, u32[]{:S(2)}) %collective-permute-start.5) | collective-permute-done | bytes 32800 | tf_op jit(solution)/shard_map/ppermute | solution.py:306
  47.0 5.6 %collective-permute-start.8 = (f32[16,128]{1,0:T(8,128)S(1)}, f32[16,128]{1,0:T(8,128)S(1)}, u32[]{:S(2)}, u32[]{:S(2)}) collective-permute-start(f32[16,128]{1,0:T(8,128)S(1)} %shard_map.134), channel_id=1, source_target_pairs={{4,0},{13,1},{22,2},{31,3},{8,4},{17,5},{26,6},{3,7},{12,8},{21,9}... | collective-permute-start | bytes 24584 | tf_op jit(solution)/shard_map/ppermute | solution.py:315
  54.0 2.2 %copy-done.3 = bf16[2,65,64,256]{3,2,1,0:T(8,128)(2,1)S(1)} copy-done((bf16[2,65,64,256]{3,2,1,0:T(8,128)(2,1)S(1)}, bf16[2,65,64,256]{3,2,1,0:T(8,128)(2,1)}, u32[]{:S(2)}) %copy-start.3) | copy-done | bytes 4259864
  56.2 1.7 %shard_map.135.refs_0_ = f32[80,256]{1,0:T(8,128)S(1)} custom-call(f32[32,128]{1,0:T(8,128)S(1)} %get-tuple-element.32.refs_0_, f32[32,128]{1,0:T(8,128)S(1)} %get-tuple-element.31.refs_1_, f32[32,128]{1,0:T(8,128)S(1)} %get-tuple-element.30.refs_2_, f32[32,128]{1,0:T(8,128)S(1)} %get-tuple-element.29.refs_3_, f32[32,128]{1,0:T(8,128)S(1)} %get-tuple-element.28.refs_4_, ...), custom_call_target="tpu_custom_call" | custom-call | tf_op jit(solution)/shard_map/pallas_call | solution.py:180
  58.6 3.5 %collective-permute-start.10 = (f32[80,256]{1,0:T(8,128)S(1)}, f32[80,256]{1,0:T(8,128)S(1)}, u32[]{:S(2)}, u32[]{:S(2)}) collective-permute-start(f32[80,256]{1,0:T(8,128)S(1)} %shard_map.135.refs_0_), channel_id=1, source_target_pairs={{0,2},{1,3},{2,0},{3,1},{4,6},{5,7},{6,4},{7,5},{8,10},{9,11},{10,... | collective-permute-start | bytes 245768 | tf_op jit(solution)/shard_map/ppermute | solution.py:293
  62.1 3.7 %collective-permute-done.10.refs_2_ = f32[80,256]{1,0:T(8,128)S(1)} collective-permute-done((f32[80,256]{1,0:T(8,128)S(1)}, f32[80,256]{1,0:T(8,128)S(1)}, u32[]{:S(2)}, u32[]{:S(2)}) %collective-permute-start.10) | collective-permute-done | bytes 81952 | tf_op jit(solution)/shard_map/ppermute | solution.py:293
  66.2 1.7 %shard_map.138 = f32[32,128]{1,0:T(8,128)S(1)} custom-call(f32[64,256]{1,0:T(8,128)S(1)} %get-tuple-element.11.gradient.field.gradient_in, bf16[2,65,64,256]{3,2,1,0:T(8,128)(2,1)S(1)} %copy-done.4, f32[144,64]{1,0:T(8,128)S(1)} %copy-done.7, f32[64,144]{1,0:T(8,128)S(1)} %copy-done.9), custom_call_target="tpu_custom_call" | custom-call | tf_op jit(solution)/shard_map/pallas_call | solution.py:180
  68.6 5.4 %all-to-all-start.2 = ((f32[8,32,128]{2,1,0:T(8,128)}), f32[8,32,128]{2,1,0:T(8,128)S(1)}, u32[]{:S(2)}, u32[]{:S(2)}) async-start(f32[8,32,128]{2,1,0:T(8,128)} %broadcast_in_dim.55), calls=%async_computation.2 | async-start | bytes 262144 | tf_op jit(solution)/shard_map/all_to_all | solution.py:299
  74.0 1.3 %collective-permute-start.13 = (f32[64,128]{1,0:T(8,128)S(1)}, f32[64,128]{1,0:T(8,128)S(1)}, u32[]{:S(2)}, u32[]{:S(2)}) collective-permute-start(f32[64,128]{1,0:T(8,128)S(1)} %get-tuple-element.41), channel_id=1, source_target_pairs={{4,0},{8,4},{12,8},{16,12},{20,16},{24,20},{28,24},{5,1},{9,5},{13... | collective-permute-start | bytes 98312 | tf_op jit(solution)/shard_map/ppermute | solution.py:306
  75.3 4.6 %collective-permute-start.12 = (f32[64,128]{1,0:T(8,128)S(1)}, f32[64,128]{1,0:T(8,128)S(1)}, u32[]{:S(2)}, u32[]{:S(2)}) collective-permute-start(f32[64,128]{1,0:T(8,128)S(1)} %get-tuple-element.42), channel_id=1, source_target_pairs={{0,4},{4,8},{8,12},{12,16},{16,20},{20,24},{24,28},{1,5},{5,9},{9,... | collective-permute-start | bytes 98312 | tf_op jit(solution)/shard_map/ppermute | solution.py:306
  80.0 1.4 %collective-permute-done.12.above = f32[64,128]{1,0:T(8,128)S(1)} collective-permute-done((f32[64,128]{1,0:T(8,128)S(1)}, f32[64,128]{1,0:T(8,128)S(1)}, u32[]{:S(2)}, u32[]{:S(2)}) %collective-permute-start.12) | collective-permute-done | bytes 32800 | tf_op jit(solution)/shard_map/ppermute | solution.py:306
  82.1 42.4 %psum.7 = f32[24]{0:T(128)S(1)} all-reduce(f32[24]{0:T(128)S(1)} %pad_maximum_fusion.3), channel_id=1, replica_groups=mesh['cell'=8,'sensor'=4] {'cell','sensor'}, use_global_device_ids=true, to_apply=%region_1.2 | all-reduce | flops 24 | bytes 192 | tf_op jit(solution)/shard_map/psum | solution.py:380
  (85 shorter events, 13.9 us)
Async XLA Ops:
  5.4 15.3 %copy-start.14 = (f32[64,64]{1,0:T(8,128)S(1)}, f32[64,64]{1,0:T(8,128)}, u32[]{:S(2)}) copy-start(f32[64,64]{1,0:T(8,128)} %param.12) | copy-start | bytes 49156
  5.4 17.1 %copy-start.12 = (f32[144,64]{1,0:T(8,128)S(1)}, f32[144,64]{1,0:T(8,128)}, u32[]{:S(2)}) copy-start(f32[144,64]{1,0:T(8,128)} %constant.29.clone.refs_11_.refs_12_) | copy-start | bytes 110596
  5.4 17.1 %copy-start.13 = (f32[64,144]{1,0:T(8,128)S(1)}, f32[64,144]{1,0:T(8,128)}, u32[]{:S(2)}) copy-start(f32[64,144]{1,0:T(8,128)} %constant.26.clone.refs_10_.refs_11_) | copy-start | bytes 110596
  5.5 22.5 %copy-start.15 = (s32[4,256]{1,0:T(4,128)S(1)}, s32[4,256]{1,0:T(4,128)}, u32[]{:S(2)}) copy-start(s32[4,256]{1,0:T(4,128)} %param.15) | copy-start | bytes 12292
  7.2 24.8 %copy-start.7 = (f32[144,64]{1,0:T(8,128)S(1)}, f32[144,64]{1,0:T(8,128)}, u32[]{:S(2)}) copy-start(f32[144,64]{1,0:T(8,128)} %constant.28.clone.plain) | copy-start | bytes 110596
  7.2 24.8 %copy-start.9 = (f32[64,144]{1,0:T(8,128)S(1)}, f32[64,144]{1,0:T(8,128)}, u32[]{:S(2)}) copy-start(f32[64,144]{1,0:T(8,128)} %constant.27.clone.weighted_t) | copy-start | bytes 110596
  7.9 14.6 %all-to-all-start = ((f32[8,32,128]{2,1,0:T(8,128)}), f32[8,32,128]{2,1,0:T(8,128)S(1)}, u32[]{:S(2)}, u32[]{:S(2)}) async-start(f32[8,32,128]{2,1,0:T(8,128)} %broadcast_in_dim.26), calls=%async_computation | async-start | bytes 262144 | tf_op jit(solution)/shard_map/all_to_all | solution.py:299
  15.4 12.6 %collective-permute-start.3 = (f32[136,128]{1,0:T(8,128)S(1)}, f32[136,128]{1,0:T(8,128)S(1)}, u32[]{:S(2)}, u32[]{:S(2)}) collective-permute-start(f32[136,128]{1,0:T(8,128)S(1)} %pad_maximum_fusion), channel_id=1, source_target_pairs={{0,4},{4,8},{8,12},{12,16},{16,20},{20,24},{24,28},{1,5},{5,9},{9,... | collective-permute-start | bytes 208904 | tf_op jit(solution)/shard_map/ppermute | solution.py:306
  19.4 8.6 %collective-permute-start.4 = (f32[136,128]{1,0:T(8,128)S(1)}, f32[136,128]{1,0:T(8,128)S(1)}, u32[]{:S(2)}, u32[]{:S(2)}) collective-permute-start(f32[136,128]{1,0:T(8,128)S(1)} %pad_maximum_fusion.1), channel_id=1, source_target_pairs={{4,0},{8,4},{12,8},{16,12},{20,16},{24,20},{28,24},{5,1},{9,5},{13... | collective-permute-start | bytes 208904 | tf_op jit(solution)/shard_map/ppermute | solution.py:306
  26.0 4.4 %collective-permute-start.2 = (f32[64,256]{1,0:T(8,128)S(1)}, f32[64,256]{1,0:T(8,128)S(1)}, u32[]{:S(2)}, u32[]{:S(2)}) collective-permute-start(f32[64,256]{1,0:T(8,128)S(1)} %shard_map.131.refs_0_), channel_id=1, source_target_pairs={{0,3},{1,2},{2,1},{3,0},{4,7},{5,6},{6,5},{7,4},{8,11},{9,10},{10,... | collective-permute-start | bytes 196616 | tf_op jit(solution)/shard_map/ppermute | solution.py:293
  26.1 5.8 %collective-permute-start.1 = (f32[64,256]{1,0:T(8,128)S(1)}, f32[64,256]{1,0:T(8,128)S(1)}, u32[]{:S(2)}, u32[]{:S(2)}) collective-permute-start(f32[64,256]{1,0:T(8,128)S(1)} %shard_map.131.refs_0_), channel_id=1, source_target_pairs={{0,2},{1,3},{2,0},{3,1},{4,6},{5,7},{6,4},{7,5},{8,10},{9,11},{10,... | collective-permute-start | bytes 196616 | tf_op jit(solution)/shard_map/ppermute | solution.py:293
  27.7 4.2 %collective-permute-start = (f32[64,256]{1,0:T(8,128)S(1)}, f32[64,256]{1,0:T(8,128)S(1)}, u32[]{:S(2)}, u32[]{:S(2)}) collective-permute-start(f32[64,256]{1,0:T(8,128)S(1)} %shard_map.131.refs_0_), channel_id=1, source_target_pairs={{0,1},{1,0},{2,3},{3,2},{4,5},{5,4},{6,7},{7,6},{8,9},{9,8},{10,11... | collective-permute-start | bytes 196616 | tf_op jit(solution)/shard_map/ppermute | solution.py:293
  34.5 18.8 %all-to-all-start.1 = ((f32[8,32,128]{2,1,0:T(8,128)}), f32[8,32,128]{2,1,0:T(8,128)S(1)}, u32[]{:S(2)}, u32[]{:S(2)}) async-start(f32[8,32,128]{2,1,0:T(8,128)} %broadcast_in_dim.53), calls=%async_computation.1 | async-start | bytes 262144 | tf_op jit(solution)/shard_map/all_to_all | solution.py:299
  39.3 6.1 %collective-permute-start.6 = (f32[64,128]{1,0:T(8,128)S(1)}, f32[64,128]{1,0:T(8,128)S(1)}, u32[]{:S(2)}, u32[]{:S(2)}) collective-permute-start(f32[64,128]{1,0:T(8,128)S(1)} %get-tuple-element.43), channel_id=1, source_target_pairs={{4,0},{8,4},{12,8},{16,12},{20,16},{24,20},{28,24},{5,1},{9,5},{13... | collective-permute-start | bytes 98312 | tf_op jit(solution)/shard_map/ppermute | solution.py:306
  40.6 6.1 %collective-permute-start.5 = (f32[64,128]{1,0:T(8,128)S(1)}, f32[64,128]{1,0:T(8,128)S(1)}, u32[]{:S(2)}, u32[]{:S(2)}) collective-permute-start(f32[64,128]{1,0:T(8,128)S(1)} %get-tuple-element.44), channel_id=1, source_target_pairs={{0,4},{4,8},{8,12},{12,16},{16,20},{20,24},{24,28},{1,5},{5,9},{9,... | collective-permute-start | bytes 98312 | tf_op jit(solution)/shard_map/ppermute | solution.py:306
  47.0 7.0 %collective-permute-start.8 = (f32[16,128]{1,0:T(8,128)S(1)}, f32[16,128]{1,0:T(8,128)S(1)}, u32[]{:S(2)}, u32[]{:S(2)}) collective-permute-start(f32[16,128]{1,0:T(8,128)S(1)} %shard_map.134), channel_id=1, source_target_pairs={{4,0},{13,1},{22,2},{31,3},{8,4},{17,5},{26,6},{3,7},{12,8},{21,9}... | collective-permute-start | bytes 24584 | tf_op jit(solution)/shard_map/ppermute | solution.py:315
  52.6 1.4 %collective-permute-start.7 = (f32[16,128]{1,0:T(8,128)S(1)}, f32[16,128]{1,0:T(8,128)S(1)}, u32[]{:S(2)}, u32[]{:S(2)}) collective-permute-start(f32[16,128]{1,0:T(8,128)S(1)} %shard_map.134), channel_id=1, source_target_pairs={{0,0},{9,1},{18,2},{27,3},{4,4},{13,5},{22,6},{31,7},{8,8},{17,9},... | collective-permute-start | bytes 24584 | tf_op jit(solution)/shard_map/ppermute | solution.py:315
  56.2 10.0 %copy-start.4 = (bf16[2,65,64,256]{3,2,1,0:T(8,128)(2,1)S(1)}, bf16[2,65,64,256]{3,2,1,0:T(8,128)(2,1)}, u32[]{:S(2)}) copy-start(bf16[2,65,64,256]{3,2,1,0:T(8,128)(2,1)} %kernel.5) | copy-start | bytes 12779524
  58.0 4.2 %collective-permute-start.11 = (f32[80,256]{1,0:T(8,128)S(1)}, f32[80,256]{1,0:T(8,128)S(1)}, u32[]{:S(2)}, u32[]{:S(2)}) collective-permute-start(f32[80,256]{1,0:T(8,128)S(1)} %shard_map.135.refs_0_), channel_id=1, source_target_pairs={{0,3},{1,2},{2,1},{3,0},{4,7},{5,6},{6,5},{7,4},{8,11},{9,10},{10,... | collective-permute-start | bytes 245768 | tf_op jit(solution)/shard_map/ppermute | solution.py:293
  58.6 7.2 %collective-permute-start.10 = (f32[80,256]{1,0:T(8,128)S(1)}, f32[80,256]{1,0:T(8,128)S(1)}, u32[]{:S(2)}, u32[]{:S(2)}) collective-permute-start(f32[80,256]{1,0:T(8,128)S(1)} %shard_map.135.refs_0_), channel_id=1, source_target_pairs={{0,2},{1,3},{2,0},{3,1},{4,6},{5,7},{6,4},{7,5},{8,10},{9,11},{10,... | collective-permute-start | bytes 245768 | tf_op jit(solution)/shard_map/ppermute | solution.py:293
  62.1 3.8 %collective-permute-start.9 = (f32[80,256]{1,0:T(8,128)S(1)}, f32[80,256]{1,0:T(8,128)S(1)}, u32[]{:S(2)}, u32[]{:S(2)}) collective-permute-start(f32[80,256]{1,0:T(8,128)S(1)} %shard_map.135.refs_0_), channel_id=1, source_target_pairs={{0,1},{1,0},{2,3},{3,2},{4,5},{5,4},{6,7},{7,6},{8,9},{9,8},{10,11... | collective-permute-start | bytes 245768 | tf_op jit(solution)/shard_map/ppermute | solution.py:293
  68.6 13.2 %all-to-all-start.2 = ((f32[8,32,128]{2,1,0:T(8,128)}), f32[8,32,128]{2,1,0:T(8,128)S(1)}, u32[]{:S(2)}, u32[]{:S(2)}) async-start(f32[8,32,128]{2,1,0:T(8,128)} %broadcast_in_dim.55), calls=%async_computation.2 | async-start | bytes 262144 | tf_op jit(solution)/shard_map/all_to_all | solution.py:299
  74.0 6.0 %collective-permute-start.13 = (f32[64,128]{1,0:T(8,128)S(1)}, f32[64,128]{1,0:T(8,128)S(1)}, u32[]{:S(2)}, u32[]{:S(2)}) collective-permute-start(f32[64,128]{1,0:T(8,128)S(1)} %get-tuple-element.41), channel_id=1, source_target_pairs={{4,0},{8,4},{12,8},{16,12},{20,16},{24,20},{28,24},{5,1},{9,5},{13... | collective-permute-start | bytes 98312 | tf_op jit(solution)/shard_map/ppermute | solution.py:306
  75.3 6.1 %collective-permute-start.12 = (f32[64,128]{1,0:T(8,128)S(1)}, f32[64,128]{1,0:T(8,128)S(1)}, u32[]{:S(2)}, u32[]{:S(2)}) collective-permute-start(f32[64,128]{1,0:T(8,128)S(1)} %get-tuple-element.42), channel_id=1, source_target_pairs={{0,4},{4,8},{8,12},{12,16},{16,20},{20,24},{24,28},{1,5},{5,9},{9,... | collective-permute-start | bytes 98312 | tf_op jit(solution)/shard_map/ppermute | solution.py:306
  (11 other events, 55.8 us)
